TPU v7x, 32 devices: a whole 2x2x4 slice. The times are simulated.
32 devices in a mesh: gx: 4 (over z), gy: 2 (over y), gz: 4 (over x, core).
Axes of the slice: x: 2, y: 2, z: 4, core: 2. Of those that a mesh axis runs over, the one named last changes fastest.
Arguments:
- density: float32 [64, 16, 1024], P('gx', 'gy', 'gz'), may hold values from 0.05 to 0.95
- voxel_kind: int32 [64, 16, 1024], P('gx', 'gy', 'gz'), may hold values from 0 to 15, as said below
Outputs:
- new_density: float32 [64, 16, 1024], P('gx', 'gy', 'gz')
- velocity: float32 [64, 16, 1024], P('gx', 'gy', 'gz')
- adjoint: float32 [64, 16, 1024], P('gx', 'gy', 'gz')
Inputs may be any that keep to these rules, and one draw needn't show every extreme that they name: `voxel_kind`: 0 to 12 mark design voxels, 13 solid, 14 inlet, 15 outlet.
All inputs are finite; a program needn't handle non-finite values.
Results may differ from a plain program's by a relative error of at most 0.0003.
Values sent between devices are 32-bit elements; how exact they have to be, the bound alone decides.
A program may use at most 128 MiB of HBM per device.

v0:
```python
import jax
import jax.numpy as jnp
from jax import lax
from jax.sharding import PartitionSpec as P

RADIUS = 6
LEVELS = 3
CYCLES = 2
COARSE_SWEEPS = 4
BISECT = 9
penalty_solid = 0.2
penalty_fluid = 0.001
convexity = 0.1
damping = 0.8
step_size = 0.1
move_limit = 0.2
volume_fraction = 0.45
epsilon = 1e-06


def with_halo(cells, sides, width):
    for axis, dim in sides:
        count = lax.axis_size(axis)
        ends = count - 1
        head = lax.slice_in_dim(cells, 0, width, axis=dim)
        tail = lax.slice_in_dim(cells, cells.shape[dim] - width, cells.shape[dim], axis=dim)
        cells = jnp.concatenate(
            [
                lax.ppermute(tail, axis, [(i, (i + 1) % count) for i in range(ends)]),
                cells,
                lax.ppermute(head, axis, [((i + 1) % count, i) for i in range(ends)]),
            ],
            axis=dim,
        )
    return cells


def smooth_axis(padded, axis_dim, length):
    result = None
    for offset in range(-RADIUS, RADIUS + 1):
        tap_term = float(RADIUS + 1 - abs(offset)) * lax.slice_in_dim(
            padded, RADIUS + offset, RADIUS + offset + length, axis=axis_dim
        )
        result = tap_term if result is None else result + tap_term
    return result


def spread(field_values):
    padded = with_halo(field_values, (("gx", 0),), RADIUS)
    field_values = smooth_axis(padded, 0, field_values.shape[0])
    padded = with_halo(field_values, (("gy", 1),), RADIUS)
    field_values = smooth_axis(padded, 1, field_values.shape[1])
    padded = with_halo(field_values, (("gz", 2),), RADIUS)
    return smooth_axis(padded, 2, field_values.shape[2])


def edge_sums(cell_count, first_index, grid_total):
    positions = first_index + jnp.arange(cell_count, dtype=jnp.int32)
    result = jnp.zeros((cell_count,), jnp.float32)
    for offset in range(-RADIUS, RADIUS + 1):
        moved = positions + offset
        inside = (moved >= 0) & (moved < grid_total)
        result = result + jnp.where(inside, float(RADIUS + 1 - abs(offset)), 0.0).astype(
            jnp.float32
        )
    return result


def neighbour_total(padded):
    beside = padded[..., 2:, 1:-1, 1:-1] + padded[..., :-2, 1:-1, 1:-1]
    beside = beside + padded[..., 1:-1, 2:, 1:-1] + padded[..., 1:-1, :-2, 1:-1]
    beside = beside + padded[..., 1:-1, 1:-1, 2:] + padded[..., 1:-1, 1:-1, :-2]
    return beside


def operate(field_values, brinkman_penalty, grid_scale):
    padded = with_halo(field_values, (("gx", 1), ("gy", 2), ("gz", 3)), 1)
    beside = neighbour_total(padded)
    return (6.0 * field_values - beside) * grid_scale + brinkman_penalty * field_values


def relax(field_values, forcing_term, brinkman_penalty, grid_scale, start_blank):
    diagonal = 6.0 * grid_scale + brinkman_penalty
    if start_blank:
        return damping * forcing_term / diagonal
    return (
        field_values
        + damping * (forcing_term - operate(field_values, brinkman_penalty, grid_scale)) / diagonal
    )


def restrict_grid(field_values):
    shape_a, shape_b, shape_c = field_values.shape[-3:]
    blocks = field_values.reshape(
        field_values.shape[:-3] + (shape_a // 2, 2, shape_b // 2, 2, shape_c // 2, 2)
    )
    return jnp.mean(blocks, axis=(-5, -3, -1))


def refine(field_values):
    return jnp.repeat(jnp.repeat(jnp.repeat(field_values, 2, axis=-3), 2, axis=-2), 2, axis=-1)


def multilevel_pass(
    field_values, forcing_term, penalty_pyramid, mesh_depth, start_blank, finest_penalty
):
    grid_scale = 0.25**mesh_depth
    brinkman_penalty = penalty_pyramid[mesh_depth]
    if mesh_depth == LEVELS - 1:
        field_values = relax(None, forcing_term, brinkman_penalty, grid_scale, True)
        for sweep_index in range(COARSE_SWEEPS - 1):
            field_values = relax(field_values, forcing_term, brinkman_penalty, grid_scale, False)
        return field_values
    field_values = relax(field_values, forcing_term, brinkman_penalty, grid_scale, start_blank)
    equation_misfit = forcing_term - operate(field_values, brinkman_penalty, grid_scale)
    coarse_update = multilevel_pass(
        None, restrict_grid(equation_misfit), penalty_pyramid, mesh_depth + 1, True, finest_penalty
    )
    field_values = field_values + refine(coarse_update)
    return relax(field_values, forcing_term, brinkman_penalty, grid_scale, False)


def compute_velocity(forcing_term, penalty_pyramid):
    field_values = None
    for vcycle_counter in range(CYCLES):
        field_values = multilevel_pass(
            field_values, forcing_term, penalty_pyramid, 0, vcycle_counter == 0, None
        )
    return field_values


def global_sums(partials):
    return lax.psum(partials, ("gx", "gy", "gz"))


def body(density, voxel_kind):
    size_x, size_y, size_z = density.shape
    total_x = size_x * lax.axis_size("gx")
    total_y = size_y * lax.axis_size("gy")
    total_z = size_z * lax.axis_size("gz")
    design = voxel_kind < 13
    solid_mask = voxel_kind == 13
    inflow_mask = voxel_kind == 14
    outflow_face = voxel_kind == 15
    sums_x = edge_sums(size_x, lax.axis_index("gx") * size_x, total_x)
    sums_y = edge_sums(size_y, lax.axis_index("gy") * size_y, total_y)
    sums_z = edge_sums(size_z, lax.axis_index("gz") * size_z, total_z)
    normal = sums_x[:, None, None] * sums_y[None, :, None] * sums_z[None, None, :]
    filtered = spread(density) / normal
    interp = penalty_solid + (penalty_fluid - penalty_solid) * filtered * (1.0 + convexity) / (
        filtered + convexity
    )
    brinkman_penalty = jnp.where(
        design, interp, jnp.where(solid_mask, penalty_solid, penalty_fluid)
    )
    penalty_pyramid = [brinkman_penalty]
    for mesh_depth in range(LEVELS - 1):
        penalty_pyramid.append(restrict_grid(penalty_pyramid[-1]))
    inflow_forcing = inflow_mask.astype(jnp.float32)
    outflow_forcing = outflow_face.astype(jnp.float32)
    velocity = compute_velocity(inflow_forcing[None], penalty_pyramid)[0]
    adjoint = compute_velocity(outflow_forcing[None], penalty_pyramid)[0]
    slope = (
        (penalty_fluid - penalty_solid)
        * (1.0 + convexity)
        * convexity
        / ((filtered + convexity) * (filtered + convexity))
    )
    gradient = jnp.where(design, adjoint * velocity * slope, 0.0)
    sensitivity = spread(gradient / normal)
    global_stats = global_sums(
        jnp.stack([jnp.sum(sensitivity * sensitivity), jnp.sum(design.astype(jnp.float32))])
    )
    cell_total = float(total_x * total_y * total_z)
    scaled = sensitivity / jnp.sqrt(global_stats[0] / cell_total + epsilon)
    target = volume_fraction * global_stats[1]
    trial_base = density - step_size * scaled
    lower_bound = jnp.maximum(0.0, density - move_limit)
    upper_bound = jnp.minimum(1.0, density + move_limit)

    def local_volume(candidate):
        return jnp.sum(
            jnp.where(design, jnp.clip(trial_base + candidate, lower_bound, upper_bound), 0.0)
        )

    start_bounds = (jnp.float32(-2.0), jnp.float32(2.0))

    def halve(step_index, bounds):
        low_end, high_end = bounds
        middle = (low_end + high_end) * 0.5
        volume = global_sums(local_volume(middle)[None])[0]
        above_target = volume > target
        return (jnp.where(above_target, low_end, middle), jnp.where(above_target, middle, high_end))

    low_end, high_end = lax.fori_loop(0, BISECT, halve, start_bounds)
    multiplier = (low_end + high_end) * 0.5
    new_density = jnp.where(
        design, jnp.clip(trial_base + multiplier, lower_bound, upper_bound), density
    )
    return (new_density, velocity, adjoint)


def solution(mesh):
    return jax.shard_map(
        body,
        mesh=mesh,
        in_specs=(P("gx", "gy", "gz"), P("gx", "gy", "gz")),
        out_specs=(P("gx", "gy", "gz"), P("gx", "gy", "gz"), P("gx", "gy", "gz")),
        check_vma=False,
    )
```

profile of v0, /device:TPU:0, one launch (start us, length us, event | category | flops | bytes accessed | tf_op | source)
XLA Modules:
  0.0 1169.2 jit_solution(6395994082612991756)
XLA Ops:
  1.5 4.9 collective-permute-start
  14.8 4.6 collective-permute-start.2
  31.1 4.5 collective-permute-start.7
  51.8 9.7 reshape.1089
  66.5 9.7 reshape.1088
  81.6 4.8 collective-permute-start.13
  104.2 4.5 collective-permute-start.19
  121.3 5.4 collective-permute-done.22
  128.1 4.8 collective-permute-start.25
  134.2 4.6 collective-permute-start.97
  154.4 4.6 collective-permute-start.31
  180.7 4.6 collective-permute-start.37
  186.8 4.7 collective-permute-start.101
  203.6 9.7 reshape.1093
  218.9 4.5 collective-permute-start.103
  240.0 4.8 collective-permute-start.109
  256.0 5.6 collective-permute-done.112
  262.9 4.8 collective-permute-start.115
  284.7 4.8 collective-permute-start.121
  292.1 4.5 collective-permute-start.123
  306.8 4.8 collective-permute-start.127
  327.9 4.8 collective-permute-start.43
  334.0 4.6 collective-permute-start.133
  344.5 4.5 collective-permute-start.135
  358.5 4.8 collective-permute-start.49
  364.9 6.6 collective-permute-start.137
  371.6 4.5 collective-permute-start.51
  390.4 4.6 collective-permute-start.55
  396.2 4.6 collective-permute-start.139
  417.5 9.7 reshape.1091
  432.6 4.5 collective-permute-start.61
  452.8 5.6 collective-permute-start.143
  461.1 4.8 collective-permute-start.67
  482.1 4.8 collective-permute-start.73
  488.2 4.6 collective-permute-start.145
  508.5 4.6 collective-permute-start.79
  534.8 4.6 collective-permute-start.85
  540.9 4.7 collective-permute-start.149
  557.6 9.7 reshape.1095
  572.9 4.5 collective-permute-start.151
  594.0 4.8 collective-permute-start.157
  610.0 5.6 collective-permute-done.160
  617.0 4.8 collective-permute-start.163
  638.7 4.8 collective-permute-start.169
  652.0 4.8 collective-permute-start.91
  665.7 4.6 collective-permute-start.175
  672.8 4.5 collective-permute-start.177
  684.5 4.5 collective-permute-start.93
  691.5 4.8 collective-permute-start.181
  699.0 4.5 collective-permute-start.183
  710.0 4.7 collective-permute-start.185
  718.6 4.8 collective-permute-start.186
  726.7 4.6 collective-permute-start.188
  742.6 47.2 %psum.14 = f32[2]{0:T(128)S(1)} all-reduce(f32[2]{0:T(128)S(1)} %pad_maximum_fusion.538), channel_id=1, replica_groups=mesh['gx'=4,'gy'=2,'gz'=4] {'gx','gy','gz'}, use_global_device_ids=true, to_apply=%region_12.13 | all-reduce | flops 2 | bytes 16 | tf_op jit(solution)/shard_map/psum | solution.py:133
  791.8 376.6 %while.12 = (s32[]{:T(128)}, f32[]{:T(128)}, f32[]{:T(128)}, f32[16,8,256]{2,1,0:T(8,128)S(1)}, f32[16,8,256]{2,1,0:T(8,128)S(1)}, /*index=5*/f32[16,8,256]{2,1,...) while((s32[]{:T(128)}, f32[]{:T(128)}, f32[]{:T(128)}, ...), condition=%wide.region_16.17_spmd, body=%wide.region_13.16_spmd.sunk | while | flops 163847 | bytes 426160 | solution.py:195
  792.5 40.4 %psum.16 = f32[]{:T(128)} all-reduce(f32[]{:T(128)} %select_reduce_fusion.2), channel_id=1, replica_groups=mesh['gx'=4,'gy'=2,'gz'=4] {'gx','gy','gz'}, use_global_device_ids=true, to_apply=%region_15.15 | all-reduce | flops 1 | bytes 8 | tf_op jit(solution)/shard_map/while/body/eval_jaxpr/psum | solution.py:133
  834.2 40.3 %psum.16 = f32[]{:T(128)} all-reduce(f32[]{:T(128)} %select_reduce_fusion.2), channel_id=1, replica_groups=mesh['gx'=4,'gy'=2,'gz'=4] {'gx','gy','gz'}, use_global_device_ids=true, to_apply=%region_15.15 | all-reduce | flops 1 | bytes 8 | tf_op jit(solution)/shard_map/while/body/eval_jaxpr/psum | solution.py:133
  875.9 40.7 %psum.16 = f32[]{:T(128)} all-reduce(f32[]{:T(128)} %select_reduce_fusion.2), channel_id=1, replica_groups=mesh['gx'=4,'gy'=2,'gz'=4] {'gx','gy','gz'}, use_global_device_ids=true, to_apply=%region_15.15 | all-reduce | flops 1 | bytes 8 | tf_op jit(solution)/shard_map/while/body/eval_jaxpr/psum | solution.py:133
  917.9 40.2 %psum.16 = f32[]{:T(128)} all-reduce(f32[]{:T(128)} %select_reduce_fusion.2), channel_id=1, replica_groups=mesh['gx'=4,'gy'=2,'gz'=4] {'gx','gy','gz'}, use_global_device_ids=true, to_apply=%region_15.15 | all-reduce | flops 1 | bytes 8 | tf_op jit(solution)/shard_map/while/body/eval_jaxpr/psum | solution.py:133
  959.6 40.8 %psum.16 = f32[]{:T(128)} all-reduce(f32[]{:T(128)} %select_reduce_fusion.2), channel_id=1, replica_groups=mesh['gx'=4,'gy'=2,'gz'=4] {'gx','gy','gz'}, use_global_device_ids=true, to_apply=%region_15.15 | all-reduce | flops 1 | bytes 8 | tf_op jit(solution)/shard_map/while/body/eval_jaxpr/psum | solution.py:133
  1001.7 40.2 %psum.16 = f32[]{:T(128)} all-reduce(f32[]{:T(128)} %select_reduce_fusion.2), channel_id=1, replica_groups=mesh['gx'=4,'gy'=2,'gz'=4] {'gx','gy','gz'}, use_global_device_ids=true, to_apply=%region_15.15 | all-reduce | flops 1 | bytes 8 | tf_op jit(solution)/shard_map/while/body/eval_jaxpr/psum | solution.py:133
  1043.2 40.8 %psum.16 = f32[]{:T(128)} all-reduce(f32[]{:T(128)} %select_reduce_fusion.2), channel_id=1, replica_groups=mesh['gx'=4,'gy'=2,'gz'=4] {'gx','gy','gz'}, use_global_device_ids=true, to_apply=%region_15.15 | all-reduce | flops 1 | bytes 8 | tf_op jit(solution)/shard_map/while/body/eval_jaxpr/psum | solution.py:133
  1085.4 40.2 %psum.16 = f32[]{:T(128)} all-reduce(f32[]{:T(128)} %select_reduce_fusion.2), channel_id=1, replica_groups=mesh['gx'=4,'gy'=2,'gz'=4] {'gx','gy','gz'}, use_global_device_ids=true, to_apply=%region_15.15 | all-reduce | flops 1 | bytes 8 | tf_op jit(solution)/shard_map/while/body/eval_jaxpr/psum | solution.py:133
  1126.9 40.8 %psum.16 = f32[]{:T(128)} all-reduce(f32[]{:T(128)} %select_reduce_fusion.2), channel_id=1, replica_groups=mesh['gx'=4,'gy'=2,'gz'=4] {'gx','gy','gz'}, use_global_device_ids=true, to_apply=%region_15.15 | all-reduce | flops 1 | bytes 8 | tf_op jit(solution)/shard_map/while/body/eval_jaxpr/psum | solution.py:133
  (665 shorter events, 467.7 us)
Async XLA Ops:
  1.5 7.9 collective-permute-start
  47.5 18.1 %collective-permute-start.10 = (f32[1,18,10,1]{3,0,2,1:T(1,128)S(1)}, f32[1,18,10,1]{3,0,2,1:T(1,128)S(1)}, u32[]{:S(2)}, u32[]{:S(2)}) collective-permute-start(f32[1,18,10,1]{3,0,2,1:T(1,128)S(1)} %get-tuple-element.139), channel_id=1, source_target_pairs={{1,0},{2,1},{3,2},{5,4},{6,5},{7,6},{9,8},{10,9},{11,10},{13,12},{... | collective-permute-start | bytes 2168 | tf_op jit(solution)/shard_map/ppermute | solution.py:31
  48.8 16.8 %collective-permute-start.11 = (f32[1,18,10,1]{3,0,2,1:T(1,128)S(1)}, f32[1,18,10,1]{3,0,2,1:T(1,128)S(1)}, u32[]{:S(2)}, u32[]{:S(2)}) collective-permute-start(f32[1,18,10,1]{3,0,2,1:T(1,128)S(1)} %get-tuple-element.140), channel_id=1, source_target_pairs={{0,1},{1,2},{2,3},{4,5},{5,6},{6,7},{8,9},{9,10},{10,11},{12,13},{... | collective-permute-start | bytes 2168 | tf_op jit(solution)/shard_map/ppermute | solution.py:29
  126.8 12.0 %collective-permute-start.24 = (f32[1,1,2,64]{3,1,2,0:T(1,128)S(1)}, f32[1,1,2,64]{3,1,2,0:T(1,128)S(1)}, u32[]{:S(2)}, u32[]{:S(2)}) collective-permute-start(f32[1,1,2,64]{3,1,2,0:T(1,128)S(1)} %get-tuple-element.344), channel_id=1, source_target_pairs={{8,0},{16,8},{24,16},{9,1},{17,9},{25,17},{10,2},{18,10},{26,18},{... | collective-permute-start | bytes 1544 | tf_op jit(solution)/shard_map/ppermute | solution.py:31
  128.1 10.7 collective-permute-start.25
  132.9 11.8 %collective-permute-start.96 = (f32[1,1,8,256]{3,2,1,0:T(8,128)S(1)}, f32[1,1,8,256]{3,2,1,0:T(8,128)S(1)}, u32[]{:S(2)}, u32[]{:S(2)}) collective-permute-start(f32[1,1,8,256]{3,2,1,0:T(8,128)S(1)} %get-tuple-element.212), channel_id=1, source_target_pairs={{8,0},{16,8},{24,16},{9,1},{17,9},{25,17},{10,2},{18,10},{26,18},{... | collective-permute-start | bytes 24584 | tf_op jit(solution)/shard_map/ppermute | solution.py:31
  134.2 10.5 collective-permute-start.97
  153.1 11.5 collective-permute-start.30
  154.4 10.3 collective-permute-start.31
  159.2 11.4 collective-permute-start.99
  179.4 12.2 %collective-permute-start.36 = (f32[1,1,4,128]{3,2,1,0:T(4,128)S(1)}, f32[1,1,4,128]{3,2,1,0:T(4,128)S(1)}, u32[]{:S(2)}, u32[]{:S(2)}) collective-permute-start(f32[1,1,4,128]{3,2,1,0:T(4,128)S(1)} %get-tuple-element.282), channel_id=1, source_target_pairs={{8,0},{16,8},{24,16},{9,1},{17,9},{25,17},{10,2},{18,10},{26,18},{... | collective-permute-start | bytes 6152 | tf_op jit(solution)/shard_map/ppermute | solution.py:31
  180.7 10.9 collective-permute-start.37
  185.5 11.9 %collective-permute-start.100 = (f32[1,18,10,1]{3,0,2,1:T(1,128)S(1)}, f32[1,18,10,1]{3,0,2,1:T(1,128)S(1)}, u32[]{:S(2)}, u32[]{:S(2)}) collective-permute-start(f32[1,18,10,1]{3,0,2,1:T(1,128)S(1)} %get-tuple-element.159), channel_id=1, source_target_pairs={{1,0},{2,1},{3,2},{5,4},{6,5},{7,6},{9,8},{10,9},{11,10},{13,12},{... | collective-permute-start | bytes 2168 | tf_op jit(solution)/shard_map/ppermute | solution.py:31
  186.8 10.7 collective-permute-start.101
  198.9 18.4 %collective-permute-start.40 = (f32[1,10,6,1]{3,0,2,1:T(1,128)S(1)}, f32[1,10,6,1]{3,0,2,1:T(1,128)S(1)}, u32[]{:S(2)}, u32[]{:S(2)}) collective-permute-start(f32[1,10,6,1]{3,0,2,1:T(1,128)S(1)} %get-tuple-element.229), channel_id=1, source_target_pairs={{1,0},{2,1},{3,2},{5,4},{6,5},{7,6},{9,8},{10,9},{11,10},{13,12},{... | collective-permute-start | bytes 728 | tf_op jit(solution)/shard_map/ppermute | solution.py:31
  200.2 17.1 %collective-permute-start.41 = (f32[1,10,6,1]{3,0,2,1:T(1,128)S(1)}, f32[1,10,6,1]{3,0,2,1:T(1,128)S(1)}, u32[]{:S(2)}, u32[]{:S(2)}) collective-permute-start(f32[1,10,6,1]{3,0,2,1:T(1,128)S(1)} %get-tuple-element.230), channel_id=1, source_target_pairs={{0,1},{1,2},{2,3},{4,5},{5,6},{6,7},{8,9},{9,10},{10,11},{12,13},{... | collective-permute-start | bytes 728 | tf_op jit(solution)/shard_map/ppermute | solution.py:29
  326.6 12.0 %collective-permute-start.42 = (f32[1,1,8,256]{3,2,1,0:T(8,128)S(1)}, f32[1,1,8,256]{3,2,1,0:T(8,128)S(1)}, u32[]{:S(2)}, u32[]{:S(2)}) collective-permute-start(f32[1,1,8,256]{3,2,1,0:T(8,128)S(1)} %get-tuple-element.198), channel_id=1, source_target_pairs={{8,0},{16,8},{24,16},{9,1},{17,9},{25,17},{10,2},{18,10},{26,18},{... | collective-permute-start | bytes 24584 | tf_op jit(solution)/shard_map/ppermute | solution.py:31
  327.9 10.7 collective-permute-start.43
  332.7 11.4 collective-permute-start.132
  334.0 10.1 collective-permute-start.133
  338.6 11.7 %collective-permute-start.45 = (f32[1,18,1,256]{3,2,1,0:T(1,128)S(1)}, f32[1,18,1,256]{3,2,1,0:T(1,128)S(1)}, u32[]{:S(2)}, u32[]{:S(2)}) collective-permute-start(f32[1,18,1,256]{3,2,1,0:T(1,128)S(1)} %get-tuple-element.168), channel_id=1, source_target_pairs={{0,4},{1,5},{2,6},{3,7},{8,12},{9,13},{10,14},{11,15},{16,20},{17,... | collective-permute-start | bytes 55304 | tf_op jit(solution)/shard_map/ppermute | solution.py:29
  342.8 7.6 collective-permute-start.44
  344.5 10.9 collective-permute-start.135
  357.2 14.3 %collective-permute-start.48 = (f32[1,1,8,256]{3,2,1,0:T(8,128)S(1)}, f32[1,1,8,256]{3,2,1,0:T(8,128)S(1)}, u32[]{:S(2)}, u32[]{:S(2)}) collective-permute-start(f32[1,1,8,256]{3,2,1,0:T(8,128)S(1)} %get-tuple-element.196), channel_id=1, source_target_pairs={{8,0},{16,8},{24,16},{9,1},{17,9},{25,17},{10,2},{18,10},{26,18},{... | collective-permute-start | bytes 24584 | tf_op jit(solution)/shard_map/ppermute | solution.py:31
  358.5 13.0 %collective-permute-start.49 = (f32[1,1,8,256]{3,2,1,0:T(8,128)S(1)}, f32[1,1,8,256]{3,2,1,0:T(8,128)S(1)}, u32[]{:S(2)}, u32[]{:S(2)}) collective-permute-start(f32[1,1,8,256]{3,2,1,0:T(8,128)S(1)} %get-tuple-element.195), channel_id=1, source_target_pairs={{0,8},{8,16},{16,24},{1,9},{9,17},{17,25},{2,10},{10,18},{18,26},{... | collective-permute-start | bytes 24584 | tf_op jit(solution)/shard_map/ppermute | solution.py:29
  363.6 13.9 %collective-permute-start.136 = (f32[1,18,10,1]{3,0,2,1:T(1,128)S(1)}, f32[1,18,10,1]{3,0,2,1:T(1,128)S(1)}, u32[]{:S(2)}, u32[]{:S(2)}) collective-permute-start(f32[1,18,10,1]{3,0,2,1:T(1,128)S(1)} %get-tuple-element.155), channel_id=1, source_target_pairs={{1,0},{2,1},{3,2},{5,4},{6,5},{7,6},{9,8},{10,9},{11,10},{13,12},{... | collective-permute-start | bytes 2168 | tf_op jit(solution)/shard_map/ppermute | solution.py:31
  364.9 12.6 %collective-permute-start.137 = (f32[1,18,10,1]{3,0,2,1:T(1,128)S(1)}, f32[1,18,10,1]{3,0,2,1:T(1,128)S(1)}, u32[]{:S(2)}, u32[]{:S(2)}) collective-permute-start(f32[1,18,10,1]{3,0,2,1:T(1,128)S(1)} %get-tuple-element.156), channel_id=1, source_target_pairs={{0,1},{1,2},{2,3},{4,5},{5,6},{6,7},{8,9},{9,10},{10,11},{12,13},{... | collective-permute-start | bytes 2168 | tf_op jit(solution)/shard_map/ppermute | solution.py:29
  389.1 11.7 %collective-permute-start.54 = (f32[1,1,8,256]{3,2,1,0:T(8,128)S(1)}, f32[1,1,8,256]{3,2,1,0:T(8,128)S(1)}, u32[]{:S(2)}, u32[]{:S(2)}) collective-permute-start(f32[1,1,8,256]{3,2,1,0:T(8,128)S(1)} %get-tuple-element.194), channel_id=1, source_target_pairs={{8,0},{16,8},{24,16},{9,1},{17,9},{25,17},{10,2},{18,10},{26,18},{... | collective-permute-start | bytes 24584 | tf_op jit(solution)/shard_map/ppermute | solution.py:31
  390.4 10.4 collective-permute-start.55
  394.9 9.3 collective-permute-start.138
  396.2 8.0 collective-permute-start.139
  409.0 7.7 collective-permute-start.58
  413.5 23.6 %collective-permute-start.141 = (f32[1,18,1,256]{3,2,1,0:T(1,128)S(1)}, f32[1,18,1,256]{3,2,1,0:T(1,128)S(1)}, u32[]{:S(2)}, u32[]{:S(2)}) collective-permute-start(f32[1,18,1,256]{3,2,1,0:T(1,128)S(1)} %get-tuple-element.176), channel_id=1, source_target_pairs={{0,4},{1,5},{2,6},{3,7},{8,12},{9,13},{10,14},{11,15},{16,20},{17,... | collective-permute-start | bytes 55304 | tf_op jit(solution)/shard_map/ppermute | solution.py:29
  415.3 21.8 %collective-permute-start.140 = (f32[1,18,1,256]{3,2,1,0:T(1,128)S(1)}, f32[1,18,1,256]{3,2,1,0:T(1,128)S(1)}, u32[]{:S(2)}, u32[]{:S(2)}) collective-permute-start(f32[1,18,1,256]{3,2,1,0:T(1,128)S(1)} %get-tuple-element.175), channel_id=1, source_target_pairs={{4,0},{5,1},{6,2},{7,3},{12,8},{13,9},{14,10},{15,11},{20,16},{21,... | collective-permute-start | bytes 55304 | tf_op jit(solution)/shard_map/ppermute | solution.py:31
  445.8 12.6 %collective-permute-start.64 = (f32[1,10,6,1]{3,0,2,1:T(1,128)S(1)}, f32[1,10,6,1]{3,0,2,1:T(1,128)S(1)}, u32[]{:S(2)}, u32[]{:S(2)}) collective-permute-start(f32[1,10,6,1]{3,0,2,1:T(1,128)S(1)} %get-tuple-element.225), channel_id=1, source_target_pairs={{1,0},{2,1},{3,2},{5,4},{6,5},{7,6},{9,8},{10,9},{11,10},{13,12},{... | collective-permute-start | bytes 728 | tf_op jit(solution)/shard_map/ppermute | solution.py:31
  447.1 11.3 collective-permute-start.65
  451.5 14.5 %collective-permute-start.142 = (f32[1,18,10,1]{3,0,2,1:T(1,128)S(1)}, f32[1,18,10,1]{3,0,2,1:T(1,128)S(1)}, u32[]{:S(2)}, u32[]{:S(2)}) collective-permute-start(f32[1,18,10,1]{3,0,2,1:T(1,128)S(1)} %get-tuple-element.151), channel_id=1, source_target_pairs={{1,0},{2,1},{3,2},{5,4},{6,5},{7,6},{9,8},{10,9},{11,10},{13,12},{... | collective-permute-start | bytes 2168 | tf_op jit(solution)/shard_map/ppermute | solution.py:31
  452.8 13.2 %collective-permute-start.143 = (f32[1,18,10,1]{3,0,2,1:T(1,128)S(1)}, f32[1,18,10,1]{3,0,2,1:T(1,128)S(1)}, u32[]{:S(2)}, u32[]{:S(2)}) collective-permute-start(f32[1,18,10,1]{3,0,2,1:T(1,128)S(1)} %get-tuple-element.152), channel_id=1, source_target_pairs={{0,1},{1,2},{2,3},{4,5},{5,6},{6,7},{8,9},{9,10},{10,11},{12,13},{... | collective-permute-start | bytes 2168 | tf_op jit(solution)/shard_map/ppermute | solution.py:29
  480.8 12.0 %collective-permute-start.72 = (f32[1,1,2,64]{3,1,2,0:T(1,128)S(1)}, f32[1,1,2,64]{3,1,2,0:T(1,128)S(1)}, u32[]{:S(2)}, u32[]{:S(2)}) collective-permute-start(f32[1,1,2,64]{3,1,2,0:T(1,128)S(1)} %get-tuple-element.338), channel_id=1, source_target_pairs={{8,0},{16,8},{24,16},{9,1},{17,9},{25,17},{10,2},{18,10},{26,18},{... | collective-permute-start | bytes 1544 | tf_op jit(solution)/shard_map/ppermute | solution.py:31
  482.1 10.7 collective-permute-start.73
  486.9 11.8 %collective-permute-start.144 = (f32[1,1,8,256]{3,2,1,0:T(8,128)S(1)}, f32[1,1,8,256]{3,2,1,0:T(8,128)S(1)}, u32[]{:S(2)}, u32[]{:S(2)}) collective-permute-start(f32[1,1,8,256]{3,2,1,0:T(8,128)S(1)} %get-tuple-element.206), channel_id=1, source_target_pairs={{8,0},{16,8},{24,16},{9,1},{17,9},{25,17},{10,2},{18,10},{26,18},{... | collective-permute-start | bytes 24584 | tf_op jit(solution)/shard_map/ppermute | solution.py:31
  488.2 10.5 collective-permute-start.145
  507.2 11.5 collective-permute-start.78
  508.5 10.3 collective-permute-start.79
  513.2 11.4 collective-permute-start.147
  533.5 12.2 %collective-permute-start.84 = (f32[1,1,4,128]{3,2,1,0:T(4,128)S(1)}, f32[1,1,4,128]{3,2,1,0:T(4,128)S(1)}, u32[]{:S(2)}, u32[]{:S(2)}) collective-permute-start(f32[1,1,4,128]{3,2,1,0:T(4,128)S(1)} %get-tuple-element.270), channel_id=1, source_target_pairs={{8,0},{16,8},{24,16},{9,1},{17,9},{25,17},{10,2},{18,10},{26,18},{... | collective-permute-start | bytes 6152 | tf_op jit(solution)/shard_map/ppermute | solution.py:31
  534.8 10.9 collective-permute-start.85
  539.6 11.9 %collective-permute-start.148 = (f32[1,18,10,1]{3,0,2,1:T(1,128)S(1)}, f32[1,18,10,1]{3,0,2,1:T(1,128)S(1)}, u32[]{:S(2)}, u32[]{:S(2)}) collective-permute-start(f32[1,18,10,1]{3,0,2,1:T(1,128)S(1)} %get-tuple-element.147), channel_id=1, source_target_pairs={{1,0},{2,1},{3,2},{5,4},{6,5},{7,6},{9,8},{10,9},{11,10},{13,12},{... | collective-permute-start | bytes 2168 | tf_op jit(solution)/shard_map/ppermute | solution.py:31
  540.9 10.7 collective-permute-start.149
  553.0 18.4 %collective-permute-start.88 = (f32[1,10,6,1]{3,0,2,1:T(1,128)S(1)}, f32[1,10,6,1]{3,0,2,1:T(1,128)S(1)}, u32[]{:S(2)}, u32[]{:S(2)}) collective-permute-start(f32[1,10,6,1]{3,0,2,1:T(1,128)S(1)} %get-tuple-element.221), channel_id=1, source_target_pairs={{1,0},{2,1},{3,2},{5,4},{6,5},{7,6},{9,8},{10,9},{11,10},{13,12},{... | collective-permute-start | bytes 728 | tf_op jit(solution)/shard_map/ppermute | solution.py:31
  554.3 17.1 %collective-permute-start.89 = (f32[1,10,6,1]{3,0,2,1:T(1,128)S(1)}, f32[1,10,6,1]{3,0,2,1:T(1,128)S(1)}, u32[]{:S(2)}, u32[]{:S(2)}) collective-permute-start(f32[1,10,6,1]{3,0,2,1:T(1,128)S(1)} %get-tuple-element.222), channel_id=1, source_target_pairs={{0,1},{1,2},{2,3},{4,5},{5,6},{6,7},{8,9},{9,10},{10,11},{12,13},{... | collective-permute-start | bytes 728 | tf_op jit(solution)/shard_map/ppermute | solution.py:29
  644.8 12.0 %collective-permute-start.170 = (f32[1,6,1,64]{3,1,2,0:T(8,128)S(1)}, f32[1,6,1,64]{3,1,2,0:T(8,128)S(1)}, u32[]{:S(2)}, u32[]{:S(2)}) collective-permute-start(f32[1,6,1,64]{3,1,2,0:T(8,128)S(1)} %get-tuple-element.324), channel_id=1, source_target_pairs={{4,0},{5,1},{6,2},{7,3},{12,8},{13,9},{14,10},{15,11},{20,16},{21,... | collective-permute-start | bytes 4616 | tf_op jit(solution)/shard_map/ppermute | solution.py:31
  646.1 10.7 collective-permute-start.171
  650.7 19.5 %collective-permute-start.90 = (f32[1,1,8,256]{3,2,1,0:T(8,128)S(1)}, f32[1,1,8,256]{3,2,1,0:T(8,128)S(1)}, u32[]{:S(2)}, u32[]{:S(2)}) collective-permute-start(f32[1,1,8,256]{3,2,1,0:T(8,128)S(1)} %get-tuple-element.192), channel_id=1, source_target_pairs={{8,0},{16,8},{24,16},{9,1},{17,9},{25,17},{10,2},{18,10},{26,18},{... | collective-permute-start | bytes 24584 | tf_op jit(solution)/shard_map/ppermute | solution.py:31
  652.0 18.2 %collective-permute-start.91 = (f32[1,1,8,256]{3,2,1,0:T(8,128)S(1)}, f32[1,1,8,256]{3,2,1,0:T(8,128)S(1)}, u32[]{:S(2)}, u32[]{:S(2)}) collective-permute-start(f32[1,1,8,256]{3,2,1,0:T(8,128)S(1)} %get-tuple-element.191), channel_id=1, source_target_pairs={{0,8},{8,16},{16,24},{1,9},{9,17},{17,25},{2,10},{10,18},{18,26},{... | collective-permute-start | bytes 24584 | tf_op jit(solution)/shard_map/ppermute | solution.py:29
  678.9 10.2 collective-permute-start.178
  680.2 8.9 collective-permute-start.179
  683.2 13.1 %collective-permute-start.92 = (f32[1,18,1,256]{3,2,1,0:T(1,128)S(1)}, f32[1,18,1,256]{3,2,1,0:T(1,128)S(1)}, u32[]{:S(2)}, u32[]{:S(2)}) collective-permute-start(f32[1,18,1,256]{3,2,1,0:T(1,128)S(1)} %get-tuple-element.162), channel_id=1, source_target_pairs={{4,0},{5,1},{6,2},{7,3},{12,8},{13,9},{14,10},{15,11},{20,16},{21,... | collective-permute-start | bytes 55304 | tf_op jit(solution)/shard_map/ppermute | solution.py:31
  684.5 11.8 %collective-permute-start.93 = (f32[1,18,1,256]{3,2,1,0:T(1,128)S(1)}, f32[1,18,1,256]{3,2,1,0:T(1,128)S(1)}, u32[]{:S(2)}, u32[]{:S(2)}) collective-permute-start(f32[1,18,1,256]{3,2,1,0:T(1,128)S(1)} %get-tuple-element.161), channel_id=1, source_target_pairs={{0,4},{1,5},{2,6},{3,7},{8,12},{9,13},{10,14},{11,15},{16,20},{17,... | collective-permute-start | bytes 55304 | tf_op jit(solution)/shard_map/ppermute | solution.py:29
  697.7 10.6 collective-permute-start.182
  699.0 9.3 collective-permute-start.183
  703.8 11.0 collective-permute-start.94
  705.1 9.7 collective-permute-start.95
  726.7 7.5 collective-permute-start.188
  (129 other events, 855.3 us)
where the time goes:
time: 1180 us; the launch traced here: 1170 us
  starting transfers between devices  516 us (44%)
  blocking collectives  411 us (35%)
  waiting for transfers between devices  110 us (9%)
  local copies, waits for them, and re-layouts  66.6 us (6%)
  other arithmetic  52.5 us (4%)
    psum x10, blocking collectives, global_sums(): return lax.psum(partials, ('gx', 'gy', 'gz'))  411 us
    ppermute x96, starting transfers between devices, with_halo(): lax.ppermute(tail, axis, [(i, (i + 1) % count) for i in range(ends)])  392 us
    ppermute x96, starting transfers between devices, with_halo(): lax.ppermute(head, axis, [((i + 1) % count, i) for i in range(ends)])  125 us
    ppermute x96, waiting for transfers between devices, with_halo(): lax.ppermute(head, axis, [((i + 1) % count, i) for i in range(ends)])  59.9 us
    reshape x9, local copies, waits for them, and re-layouts, restrict_grid(): field_values.reshape(field_values.shape[:-3] + (shape_a // 2, 2, shape_b...  52.7 us
    ppermute x96, waiting for transfers between devices, with_halo(): lax.ppermute(tail, axis, [(i, (i + 1) % count) for i in range(ends)])  50.4 us
  transfers between devices with their start and end apart: 192, of which 64 were waited for; matrix products, arithmetic and copies ran while one was open for 6% of the time, Pallas kernels for 0%

commit v1 on v0

--- a/solution.py
+++ b/solution.py
@@ -1,3 +1,4 @@
+import functools
 import jax
 import jax.numpy as jnp
 from jax import lax
@@ -16,6 +17,14 @@
 move_limit = 0.2
 volume_fraction = 0.45
 epsilon = 1e-06
+
+
+def fit_lanes(z, a_name, link_axis):
+    w2 = lax.psum(z, a_name)
+    return lax.psum(w2, link_axis)
+
+
+apply_field = functools.partial(fit_lanes, a_name=("gy", "gz"), link_axis="gx")
 
 
 def with_halo(cells, sides, width):
@@ -130,7 +139,7 @@
 
 
 def global_sums(partials):
-    return lax.psum(partials, ("gx", "gy", "gz"))
+    return apply_field(partials)
 
 
 def body(density, voxel_kind):

time: 1180 us -> 1000 us (0.85)
  blocking collectives: 411 us -> 231 us
    psum x10 -> x20, blocking collectives: 411 us -> 231 us  [the longest x10 129 us: fit_lanes(): w2 = lax.psum(z, a_name)]
  transfers between devices with their start and end apart: 192 -> 192, of which waited for: 64 -> 64; matrix products, arithmetic and copies ran while one was open for 6% -> 7% of each run, Pallas kernels for 0% -> 0%
where the time goes in v1:
time: 1000 us; the launch traced here: 988 us
  starting transfers between devices  516 us (52%)
  blocking collectives  231 us (23%)
  waiting for transfers between devices  110 us (11%)
  local copies, waits for them, and re-layouts  66.5 us (7%)
  other arithmetic  51.7 us (5%)
    ppermute x96, starting transfers between devices, with_halo(): lax.ppermute(tail, axis, [(i, (i + 1) % count) for i in range(ends)])  392 us
    psum x10, blocking collectives, fit_lanes(): w2 = lax.psum(z, a_name)  129 us
    ppermute x96, starting transfers between devices, with_halo(): lax.ppermute(head, axis, [((i + 1) % count, i) for i in range(ends)])  125 us
    psum x10, blocking collectives, fit_lanes(): return lax.psum(w2, link_axis)  102 us
    ppermute x96, waiting for transfers between devices, with_halo(): lax.ppermute(head, axis, [((i + 1) % count, i) for i in range(ends)])  60 us
    reshape x9, local copies, waits for them, and re-layouts, restrict_grid(): field_values.reshape(field_values.shape[:-3] + (shape_a // 2, 2, shape_b...  52.6 us
    ppermute x96, waiting for transfers between devices, with_halo(): lax.ppermute(tail, axis, [(i, (i + 1) % count) for i in range(ends)])  50.4 us
    reduce_sum x10, other arithmetic, restrict_grid(): return jnp.mean(blocks, axis=(-5, -3, -1))  20.9 us
  transfers between devices with their start and end apart: 192, of which 64 were waited for; matrix products, arithmetic and copies ran while one was open for 7% of the time, Pallas kernels for 0%

profile of v1, /device:TPU:0, one launch (start us, length us, event | category | flops | bytes accessed | tf_op | source)
XLA Modules:
  0.0 987.6 jit_solution(3447951656686136035)
XLA Ops:
  1.5 4.9 collective-permute-start
  14.8 4.6 collective-permute-start.2
  31.1 4.5 collective-permute-start.7
  51.8 9.7 reshape.1089
  66.5 9.7 reshape.1088
  81.6 4.8 collective-permute-start.13
  121.3 5.4 collective-permute-done.22
  128.0 4.8 collective-permute-start.25
  134.2 4.6 collective-permute-start.97
  154.4 4.6 collective-permute-start.31
  180.7 4.6 collective-permute-start.37
  186.8 4.7 collective-permute-start.101
  203.6 9.7 reshape.1093
  240.0 4.8 collective-permute-start.109
  255.9 5.6 collective-permute-done.112
  262.9 4.8 collective-permute-start.115
  284.7 4.8 collective-permute-start.121
  306.8 4.8 collective-permute-start.127
  327.8 4.8 collective-permute-start.43
  334.0 4.6 collective-permute-start.133
  358.5 4.8 collective-permute-start.49
  364.8 6.6 collective-permute-start.137
  390.4 4.6 collective-permute-start.55
  396.2 4.6 collective-permute-start.139
  417.5 9.7 reshape.1091
  452.7 5.6 collective-permute-start.143
  461.1 4.8 collective-permute-start.67
  482.1 4.8 collective-permute-start.73
  488.2 4.6 collective-permute-start.145
  508.5 4.6 collective-permute-start.79
  534.7 4.6 collective-permute-start.85
  540.8 4.7 collective-permute-start.149
  557.6 9.7 reshape.1095
  594.0 4.8 collective-permute-start.157
  610.0 5.6 collective-permute-done.160
  616.9 4.8 collective-permute-start.163
  638.7 4.8 collective-permute-start.169
  652.0 4.8 collective-permute-start.91
  665.6 4.6 collective-permute-start.175
  691.4 4.8 collective-permute-start.181
  710.0 4.7 collective-permute-start.185
  718.6 4.8 collective-permute-start.186
  726.6 4.6 collective-permute-start.188
  742.4 17.4 %psum.28 = f32[2]{0:T(128)S(1)} all-reduce(f32[2]{0:T(128)S(1)} %pad_maximum_fusion.538), channel_id=1, replica_groups=mesh['gx'=4,'gy'=2,'gz'=4] {'gy','gz'}, use_global_device_ids=true, to_apply=%region_12.13 | all-reduce | flops 2 | bytes 16 | tf_op jit(solution)/shard_map/psum | solution.py:23
  759.8 13.6 %psum.29 = f32[2]{0:T(128)S(1)} all-reduce(f32[2]{0:T(128)S(1)} %psum.28), channel_id=1, replica_groups=mesh['gx'=4,'gy'=2,'gz'=4] {'gx'}, use_global_device_ids=true, to_apply=%region_13.14 | all-reduce | flops 2 | bytes 16 | tf_op jit(solution)/shard_map/psum | solution.py:24
  775.2 211.5 %while.12 = (s32[]{:T(128)}, f32[]{:T(128)}, f32[]{:T(128)}, f32[16,8,256]{2,1,0:T(8,128)S(1)}, f32[16,8,256]{2,1,0:T(8,128)S(1)}, /*index=5*/f32[16,8,256]{2,1,...) while((s32[]{:T(128)}, f32[]{:T(128)}, f32[]{:T(128)}, ...), condition=%wide.region_18.19_spmd, body=%wide.region_14.18_spmd.sunk | while | flops 163848 | bytes 426168 | solution.py:204
  775.8 12.4 %psum.32 = f32[1]{0:T(128)} all-reduce(f32[1]{0:T(128)} %bitcast.408), channel_id=1, replica_groups=mesh['gx'=4,'gy'=2,'gz'=4] {'gy','gz'}, use_global_device_ids=true, to_apply=%region_16.16 | all-reduce | flops 1 | bytes 8 | tf_op jit(solution)/shard_map/while/body/eval_jaxpr/psum | solution.py:23
  788.2 9.0 psum.33
  798.4 12.4 %psum.32 = f32[1]{0:T(128)} all-reduce(f32[1]{0:T(128)} %bitcast.408), channel_id=1, replica_groups=mesh['gx'=4,'gy'=2,'gz'=4] {'gy','gz'}, use_global_device_ids=true, to_apply=%region_16.16 | all-reduce | flops 1 | bytes 8 | tf_op jit(solution)/shard_map/while/body/eval_jaxpr/psum | solution.py:23
  810.8 11.0 %psum.33 = f32[]{:T(128)} all-reduce(f32[]{:T(128)} %bitcast.409), channel_id=1, replica_groups=mesh['gx'=4,'gy'=2,'gz'=4] {'gx'}, use_global_device_ids=true, to_apply=%region_17.17 | all-reduce | flops 1 | bytes 8 | tf_op jit(solution)/shard_map/while/body/eval_jaxpr/psum | solution.py:24
  823.1 12.4 %psum.32 = f32[1]{0:T(128)} all-reduce(f32[1]{0:T(128)} %bitcast.408), channel_id=1, replica_groups=mesh['gx'=4,'gy'=2,'gz'=4] {'gy','gz'}, use_global_device_ids=true, to_apply=%region_16.16 | all-reduce | flops 1 | bytes 8 | tf_op jit(solution)/shard_map/while/body/eval_jaxpr/psum | solution.py:23
  835.4 9.0 psum.33
  845.7 12.4 %psum.32 = f32[1]{0:T(128)} all-reduce(f32[1]{0:T(128)} %bitcast.408), channel_id=1, replica_groups=mesh['gx'=4,'gy'=2,'gz'=4] {'gy','gz'}, use_global_device_ids=true, to_apply=%region_16.16 | all-reduce | flops 1 | bytes 8 | tf_op jit(solution)/shard_map/while/body/eval_jaxpr/psum | solution.py:23
  858.1 11.0 %psum.33 = f32[]{:T(128)} all-reduce(f32[]{:T(128)} %bitcast.409), channel_id=1, replica_groups=mesh['gx'=4,'gy'=2,'gz'=4] {'gx'}, use_global_device_ids=true, to_apply=%region_17.17 | all-reduce | flops 1 | bytes 8 | tf_op jit(solution)/shard_map/while/body/eval_jaxpr/psum | solution.py:24
  870.3 12.4 %psum.32 = f32[1]{0:T(128)} all-reduce(f32[1]{0:T(128)} %bitcast.408), channel_id=1, replica_groups=mesh['gx'=4,'gy'=2,'gz'=4] {'gy','gz'}, use_global_device_ids=true, to_apply=%region_16.16 | all-reduce | flops 1 | bytes 8 | tf_op jit(solution)/shard_map/while/body/eval_jaxpr/psum | solution.py:23
  882.7 9.0 psum.33
  892.9 12.4 %psum.32 = f32[1]{0:T(128)} all-reduce(f32[1]{0:T(128)} %bitcast.408), channel_id=1, replica_groups=mesh['gx'=4,'gy'=2,'gz'=4] {'gy','gz'}, use_global_device_ids=true, to_apply=%region_16.16 | all-reduce | flops 1 | bytes 8 | tf_op jit(solution)/shard_map/while/body/eval_jaxpr/psum | solution.py:23
  905.3 11.0 %psum.33 = f32[]{:T(128)} all-reduce(f32[]{:T(128)} %bitcast.409), channel_id=1, replica_groups=mesh['gx'=4,'gy'=2,'gz'=4] {'gx'}, use_global_device_ids=true, to_apply=%region_17.17 | all-reduce | flops 1 | bytes 8 | tf_op jit(solution)/shard_map/while/body/eval_jaxpr/psum | solution.py:24
  917.5 12.4 %psum.32 = f32[1]{0:T(128)} all-reduce(f32[1]{0:T(128)} %bitcast.408), channel_id=1, replica_groups=mesh['gx'=4,'gy'=2,'gz'=4] {'gy','gz'}, use_global_device_ids=true, to_apply=%region_16.16 | all-reduce | flops 1 | bytes 8 | tf_op jit(solution)/shard_map/while/body/eval_jaxpr/psum | solution.py:23
  929.9 9.0 psum.33
  940.1 12.4 %psum.32 = f32[1]{0:T(128)} all-reduce(f32[1]{0:T(128)} %bitcast.408), channel_id=1, replica_groups=mesh['gx'=4,'gy'=2,'gz'=4] {'gy','gz'}, use_global_device_ids=true, to_apply=%region_16.16 | all-reduce | flops 1 | bytes 8 | tf_op jit(solution)/shard_map/while/body/eval_jaxpr/psum | solution.py:23
  952.5 11.0 %psum.33 = f32[]{:T(128)} all-reduce(f32[]{:T(128)} %bitcast.409), channel_id=1, replica_groups=mesh['gx'=4,'gy'=2,'gz'=4] {'gx'}, use_global_device_ids=true, to_apply=%region_17.17 | all-reduce | flops 1 | bytes 8 | tf_op jit(solution)/shard_map/while/body/eval_jaxpr/psum | solution.py:24
  964.7 12.4 %psum.32 = f32[1]{0:T(128)} all-reduce(f32[1]{0:T(128)} %bitcast.408), channel_id=1, replica_groups=mesh['gx'=4,'gy'=2,'gz'=4] {'gy','gz'}, use_global_device_ids=true, to_apply=%region_16.16 | all-reduce | flops 1 | bytes 8 | tf_op jit(solution)/shard_map/while/body/eval_jaxpr/psum | solution.py:23
  977.1 9.0 psum.33
  (675 shorter events, 512.4 us)
Async XLA Ops:
  1.5 7.8 collective-permute-start
  47.5 18.1 %collective-permute-start.10 = (f32[1,18,10,1]{3,0,2,1:T(1,128)S(1)}, f32[1,18,10,1]{3,0,2,1:T(1,128)S(1)}, u32[]{:S(2)}, u32[]{:S(2)}) collective-permute-start(f32[1,18,10,1]{3,0,2,1:T(1,128)S(1)} %get-tuple-element.139), channel_id=1, source_target_pairs={{1,0},{2,1},{3,2},{5,4},{6,5},{7,6},{9,8},{10,9},{11,10},{13,12},{... | collective-permute-start | bytes 2168 | tf_op jit(solution)/shard_map/ppermute | solution.py:40
  48.8 16.8 %collective-permute-start.11 = (f32[1,18,10,1]{3,0,2,1:T(1,128)S(1)}, f32[1,18,10,1]{3,0,2,1:T(1,128)S(1)}, u32[]{:S(2)}, u32[]{:S(2)}) collective-permute-start(f32[1,18,10,1]{3,0,2,1:T(1,128)S(1)} %get-tuple-element.140), channel_id=1, source_target_pairs={{0,1},{1,2},{2,3},{4,5},{5,6},{6,7},{8,9},{9,10},{10,11},{12,13},{... | collective-permute-start | bytes 2168 | tf_op jit(solution)/shard_map/ppermute | solution.py:38
  126.7 12.0 %collective-permute-start.24 = (f32[1,1,2,64]{3,1,2,0:T(1,128)S(1)}, f32[1,1,2,64]{3,1,2,0:T(1,128)S(1)}, u32[]{:S(2)}, u32[]{:S(2)}) collective-permute-start(f32[1,1,2,64]{3,1,2,0:T(1,128)S(1)} %get-tuple-element.344), channel_id=1, source_target_pairs={{8,0},{16,8},{24,16},{9,1},{17,9},{25,17},{10,2},{18,10},{26,18},{... | collective-permute-start | bytes 1544 | tf_op jit(solution)/shard_map/ppermute | solution.py:40
  128.0 10.7 %collective-permute-start.25 = (f32[1,1,2,64]{3,1,2,0:T(1,128)S(1)}, f32[1,1,2,64]{3,1,2,0:T(1,128)S(1)}, u32[]{:S(2)}, u32[]{:S(2)}) collective-permute-start(f32[1,1,2,64]{3,1,2,0:T(1,128)S(1)} %get-tuple-element.343), channel_id=1, source_target_pairs={{0,8},{8,16},{16,24},{1,9},{9,17},{17,25},{2,10},{10,18},{18,26},{... | collective-permute-start | bytes 1544 | tf_op jit(solution)/shard_map/ppermute | solution.py:38
  132.9 11.8 %collective-permute-start.96 = (f32[1,1,8,256]{3,2,1,0:T(8,128)S(1)}, f32[1,1,8,256]{3,2,1,0:T(8,128)S(1)}, u32[]{:S(2)}, u32[]{:S(2)}) collective-permute-start(f32[1,1,8,256]{3,2,1,0:T(8,128)S(1)} %get-tuple-element.212), channel_id=1, source_target_pairs={{8,0},{16,8},{24,16},{9,1},{17,9},{25,17},{10,2},{18,10},{26,18},{... | collective-permute-start | bytes 24584 | tf_op jit(solution)/shard_map/ppermute | solution.py:40
  134.2 10.5 %collective-permute-start.97 = (f32[1,1,8,256]{3,2,1,0:T(8,128)S(1)}, f32[1,1,8,256]{3,2,1,0:T(8,128)S(1)}, u32[]{:S(2)}, u32[]{:S(2)}) collective-permute-start(f32[1,1,8,256]{3,2,1,0:T(8,128)S(1)} %get-tuple-element.211), channel_id=1, source_target_pairs={{0,8},{8,16},{16,24},{1,9},{9,17},{17,25},{2,10},{10,18},{18,26},{... | collective-permute-start | bytes 24584 | tf_op jit(solution)/shard_map/ppermute | solution.py:38
  153.1 11.5 %collective-permute-start.30 = (f32[1,1,2,64]{3,1,2,0:T(1,128)S(1)}, f32[1,1,2,64]{3,1,2,0:T(1,128)S(1)}, u32[]{:S(2)}, u32[]{:S(2)}) collective-permute-start(f32[1,1,2,64]{3,1,2,0:T(1,128)S(1)} %get-tuple-element.342), channel_id=1, source_target_pairs={{8,0},{16,8},{24,16},{9,1},{17,9},{25,17},{10,2},{18,10},{26,18},{... | collective-permute-start | bytes 1544 | tf_op jit(solution)/shard_map/ppermute | solution.py:40
  154.4 10.3 %collective-permute-start.31 = (f32[1,1,2,64]{3,1,2,0:T(1,128)S(1)}, f32[1,1,2,64]{3,1,2,0:T(1,128)S(1)}, u32[]{:S(2)}, u32[]{:S(2)}) collective-permute-start(f32[1,1,2,64]{3,1,2,0:T(1,128)S(1)} %get-tuple-element.341), channel_id=1, source_target_pairs={{0,8},{8,16},{16,24},{1,9},{9,17},{17,25},{2,10},{10,18},{18,26},{... | collective-permute-start | bytes 1544 | tf_op jit(solution)/shard_map/ppermute | solution.py:38
  159.2 11.4 %collective-permute-start.99 = (f32[1,18,1,256]{3,2,1,0:T(1,128)S(1)}, f32[1,18,1,256]{3,2,1,0:T(1,128)S(1)}, u32[]{:S(2)}, u32[]{:S(2)}) collective-permute-start(f32[1,18,1,256]{3,2,1,0:T(1,128)S(1)} %get-tuple-element.180), channel_id=1, source_target_pairs={{0,4},{1,5},{2,6},{3,7},{8,12},{9,13},{10,14},{11,15},{16,20},{17,... | collective-permute-start | bytes 55304 | tf_op jit(solution)/shard_map/ppermute | solution.py:38
  179.4 12.2 %collective-permute-start.36 = (f32[1,1,4,128]{3,2,1,0:T(4,128)S(1)}, f32[1,1,4,128]{3,2,1,0:T(4,128)S(1)}, u32[]{:S(2)}, u32[]{:S(2)}) collective-permute-start(f32[1,1,4,128]{3,2,1,0:T(4,128)S(1)} %get-tuple-element.282), channel_id=1, source_target_pairs={{8,0},{16,8},{24,16},{9,1},{17,9},{25,17},{10,2},{18,10},{26,18},{... | collective-permute-start | bytes 6152 | tf_op jit(solution)/shard_map/ppermute | solution.py:40
  180.7 10.9 %collective-permute-start.37 = (f32[1,1,4,128]{3,2,1,0:T(4,128)S(1)}, f32[1,1,4,128]{3,2,1,0:T(4,128)S(1)}, u32[]{:S(2)}, u32[]{:S(2)}) collective-permute-start(f32[1,1,4,128]{3,2,1,0:T(4,128)S(1)} %get-tuple-element.281), channel_id=1, source_target_pairs={{0,8},{8,16},{16,24},{1,9},{9,17},{17,25},{2,10},{10,18},{18,26},{... | collective-permute-start | bytes 6152 | tf_op jit(solution)/shard_map/ppermute | solution.py:38
  185.5 11.9 %collective-permute-start.100 = (f32[1,18,10,1]{3,0,2,1:T(1,128)S(1)}, f32[1,18,10,1]{3,0,2,1:T(1,128)S(1)}, u32[]{:S(2)}, u32[]{:S(2)}) collective-permute-start(f32[1,18,10,1]{3,0,2,1:T(1,128)S(1)} %get-tuple-element.159), channel_id=1, source_target_pairs={{1,0},{2,1},{3,2},{5,4},{6,5},{7,6},{9,8},{10,9},{11,10},{13,12},{... | collective-permute-start | bytes 2168 | tf_op jit(solution)/shard_map/ppermute | solution.py:40
  186.8 10.7 %collective-permute-start.101 = (f32[1,18,10,1]{3,0,2,1:T(1,128)S(1)}, f32[1,18,10,1]{3,0,2,1:T(1,128)S(1)}, u32[]{:S(2)}, u32[]{:S(2)}) collective-permute-start(f32[1,18,10,1]{3,0,2,1:T(1,128)S(1)} %get-tuple-element.160), channel_id=1, source_target_pairs={{0,1},{1,2},{2,3},{4,5},{5,6},{6,7},{8,9},{9,10},{10,11},{12,13},{... | collective-permute-start | bytes 2168 | tf_op jit(solution)/shard_map/ppermute | solution.py:38
  198.9 18.4 %collective-permute-start.40 = (f32[1,10,6,1]{3,0,2,1:T(1,128)S(1)}, f32[1,10,6,1]{3,0,2,1:T(1,128)S(1)}, u32[]{:S(2)}, u32[]{:S(2)}) collective-permute-start(f32[1,10,6,1]{3,0,2,1:T(1,128)S(1)} %get-tuple-element.229), channel_id=1, source_target_pairs={{1,0},{2,1},{3,2},{5,4},{6,5},{7,6},{9,8},{10,9},{11,10},{13,12},{... | collective-permute-start | bytes 728 | tf_op jit(solution)/shard_map/ppermute | solution.py:40
  200.2 17.1 %collective-permute-start.41 = (f32[1,10,6,1]{3,0,2,1:T(1,128)S(1)}, f32[1,10,6,1]{3,0,2,1:T(1,128)S(1)}, u32[]{:S(2)}, u32[]{:S(2)}) collective-permute-start(f32[1,10,6,1]{3,0,2,1:T(1,128)S(1)} %get-tuple-element.230), channel_id=1, source_target_pairs={{0,1},{1,2},{2,3},{4,5},{5,6},{6,7},{8,9},{9,10},{10,11},{12,13},{... | collective-permute-start | bytes 728 | tf_op jit(solution)/shard_map/ppermute | solution.py:38
  326.5 12.0 %collective-permute-start.42 = (f32[1,1,8,256]{3,2,1,0:T(8,128)S(1)}, f32[1,1,8,256]{3,2,1,0:T(8,128)S(1)}, u32[]{:S(2)}, u32[]{:S(2)}) collective-permute-start(f32[1,1,8,256]{3,2,1,0:T(8,128)S(1)} %get-tuple-element.198), channel_id=1, source_target_pairs={{8,0},{16,8},{24,16},{9,1},{17,9},{25,17},{10,2},{18,10},{26,18},{... | collective-permute-start | bytes 24584 | tf_op jit(solution)/shard_map/ppermute | solution.py:40
  327.8 10.7 %collective-permute-start.43 = (f32[1,1,8,256]{3,2,1,0:T(8,128)S(1)}, f32[1,1,8,256]{3,2,1,0:T(8,128)S(1)}, u32[]{:S(2)}, u32[]{:S(2)}) collective-permute-start(f32[1,1,8,256]{3,2,1,0:T(8,128)S(1)} %get-tuple-element.197), channel_id=1, source_target_pairs={{0,8},{8,16},{16,24},{1,9},{9,17},{17,25},{2,10},{10,18},{18,26},{... | collective-permute-start | bytes 24584 | tf_op jit(solution)/shard_map/ppermute | solution.py:38
  332.7 11.4 %collective-permute-start.132 = (f32[1,1,8,256]{3,2,1,0:T(8,128)S(1)}, f32[1,1,8,256]{3,2,1,0:T(8,128)S(1)}, u32[]{:S(2)}, u32[]{:S(2)}) collective-permute-start(f32[1,1,8,256]{3,2,1,0:T(8,128)S(1)} %get-tuple-element.210), channel_id=1, source_target_pairs={{8,0},{16,8},{24,16},{9,1},{17,9},{25,17},{10,2},{18,10},{26,18},{... | collective-permute-start | bytes 24584 | tf_op jit(solution)/shard_map/ppermute | solution.py:40
  334.0 10.1 %collective-permute-start.133 = (f32[1,1,8,256]{3,2,1,0:T(8,128)S(1)}, f32[1,1,8,256]{3,2,1,0:T(8,128)S(1)}, u32[]{:S(2)}, u32[]{:S(2)}) collective-permute-start(f32[1,1,8,256]{3,2,1,0:T(8,128)S(1)} %get-tuple-element.209), channel_id=1, source_target_pairs={{0,8},{8,16},{16,24},{1,9},{9,17},{17,25},{2,10},{10,18},{18,26},{... | collective-permute-start | bytes 24584 | tf_op jit(solution)/shard_map/ppermute | solution.py:38
  338.6 11.7 %collective-permute-start.45 = (f32[1,18,1,256]{3,2,1,0:T(1,128)S(1)}, f32[1,18,1,256]{3,2,1,0:T(1,128)S(1)}, u32[]{:S(2)}, u32[]{:S(2)}) collective-permute-start(f32[1,18,1,256]{3,2,1,0:T(1,128)S(1)} %get-tuple-element.168), channel_id=1, source_target_pairs={{0,4},{1,5},{2,6},{3,7},{8,12},{9,13},{10,14},{11,15},{16,20},{17,... | collective-permute-start | bytes 55304 | tf_op jit(solution)/shard_map/ppermute | solution.py:38
  342.8 7.6 collective-permute-start.44
  344.5 10.9 %collective-permute-start.135 = (f32[1,18,1,256]{3,2,1,0:T(1,128)S(1)}, f32[1,18,1,256]{3,2,1,0:T(1,128)S(1)}, u32[]{:S(2)}, u32[]{:S(2)}) collective-permute-start(f32[1,18,1,256]{3,2,1,0:T(1,128)S(1)} %get-tuple-element.178), channel_id=1, source_target_pairs={{0,4},{1,5},{2,6},{3,7},{8,12},{9,13},{10,14},{11,15},{16,20},{17,... | collective-permute-start | bytes 55304 | tf_op jit(solution)/shard_map/ppermute | solution.py:38
  357.2 14.3 %collective-permute-start.48 = (f32[1,1,8,256]{3,2,1,0:T(8,128)S(1)}, f32[1,1,8,256]{3,2,1,0:T(8,128)S(1)}, u32[]{:S(2)}, u32[]{:S(2)}) collective-permute-start(f32[1,1,8,256]{3,2,1,0:T(8,128)S(1)} %get-tuple-element.196), channel_id=1, source_target_pairs={{8,0},{16,8},{24,16},{9,1},{17,9},{25,17},{10,2},{18,10},{26,18},{... | collective-permute-start | bytes 24584 | tf_op jit(solution)/shard_map/ppermute | solution.py:40
  358.5 13.0 %collective-permute-start.49 = (f32[1,1,8,256]{3,2,1,0:T(8,128)S(1)}, f32[1,1,8,256]{3,2,1,0:T(8,128)S(1)}, u32[]{:S(2)}, u32[]{:S(2)}) collective-permute-start(f32[1,1,8,256]{3,2,1,0:T(8,128)S(1)} %get-tuple-element.195), channel_id=1, source_target_pairs={{0,8},{8,16},{16,24},{1,9},{9,17},{17,25},{2,10},{10,18},{18,26},{... | collective-permute-start | bytes 24584 | tf_op jit(solution)/shard_map/ppermute | solution.py:38
  363.5 13.9 %collective-permute-start.136 = (f32[1,18,10,1]{3,0,2,1:T(1,128)S(1)}, f32[1,18,10,1]{3,0,2,1:T(1,128)S(1)}, u32[]{:S(2)}, u32[]{:S(2)}) collective-permute-start(f32[1,18,10,1]{3,0,2,1:T(1,128)S(1)} %get-tuple-element.155), channel_id=1, source_target_pairs={{1,0},{2,1},{3,2},{5,4},{6,5},{7,6},{9,8},{10,9},{11,10},{13,12},{... | collective-permute-start | bytes 2168 | tf_op jit(solution)/shard_map/ppermute | solution.py:40
  364.8 12.6 %collective-permute-start.137 = (f32[1,18,10,1]{3,0,2,1:T(1,128)S(1)}, f32[1,18,10,1]{3,0,2,1:T(1,128)S(1)}, u32[]{:S(2)}, u32[]{:S(2)}) collective-permute-start(f32[1,18,10,1]{3,0,2,1:T(1,128)S(1)} %get-tuple-element.156), channel_id=1, source_target_pairs={{0,1},{1,2},{2,3},{4,5},{5,6},{6,7},{8,9},{9,10},{10,11},{12,13},{... | collective-permute-start | bytes 2168 | tf_op jit(solution)/shard_map/ppermute | solution.py:38
  389.1 11.7 %collective-permute-start.54 = (f32[1,1,8,256]{3,2,1,0:T(8,128)S(1)}, f32[1,1,8,256]{3,2,1,0:T(8,128)S(1)}, u32[]{:S(2)}, u32[]{:S(2)}) collective-permute-start(f32[1,1,8,256]{3,2,1,0:T(8,128)S(1)} %get-tuple-element.194), channel_id=1, source_target_pairs={{8,0},{16,8},{24,16},{9,1},{17,9},{25,17},{10,2},{18,10},{26,18},{... | collective-permute-start | bytes 24584 | tf_op jit(solution)/shard_map/ppermute | solution.py:40
  390.4 10.4 %collective-permute-start.55 = (f32[1,1,8,256]{3,2,1,0:T(8,128)S(1)}, f32[1,1,8,256]{3,2,1,0:T(8,128)S(1)}, u32[]{:S(2)}, u32[]{:S(2)}) collective-permute-start(f32[1,1,8,256]{3,2,1,0:T(8,128)S(1)} %get-tuple-element.193), channel_id=1, source_target_pairs={{0,8},{8,16},{16,24},{1,9},{9,17},{17,25},{2,10},{10,18},{18,26},{... | collective-permute-start | bytes 24584 | tf_op jit(solution)/shard_map/ppermute | solution.py:38
  394.9 9.3 collective-permute-start.138
  396.2 8.0 collective-permute-start.139
  408.9 7.7 collective-permute-start.58
  413.5 23.6 %collective-permute-start.141 = (f32[1,18,1,256]{3,2,1,0:T(1,128)S(1)}, f32[1,18,1,256]{3,2,1,0:T(1,128)S(1)}, u32[]{:S(2)}, u32[]{:S(2)}) collective-permute-start(f32[1,18,1,256]{3,2,1,0:T(1,128)S(1)} %get-tuple-element.176), channel_id=1, source_target_pairs={{0,4},{1,5},{2,6},{3,7},{8,12},{9,13},{10,14},{11,15},{16,20},{17,... | collective-permute-start | bytes 55304 | tf_op jit(solution)/shard_map/ppermute | solution.py:38
  415.3 21.8 %collective-permute-start.140 = (f32[1,18,1,256]{3,2,1,0:T(1,128)S(1)}, f32[1,18,1,256]{3,2,1,0:T(1,128)S(1)}, u32[]{:S(2)}, u32[]{:S(2)}) collective-permute-start(f32[1,18,1,256]{3,2,1,0:T(1,128)S(1)} %get-tuple-element.175), channel_id=1, source_target_pairs={{4,0},{5,1},{6,2},{7,3},{12,8},{13,9},{14,10},{15,11},{20,16},{21,... | collective-permute-start | bytes 55304 | tf_op jit(solution)/shard_map/ppermute | solution.py:40
  445.7 12.6 %collective-permute-start.64 = (f32[1,10,6,1]{3,0,2,1:T(1,128)S(1)}, f32[1,10,6,1]{3,0,2,1:T(1,128)S(1)}, u32[]{:S(2)}, u32[]{:S(2)}) collective-permute-start(f32[1,10,6,1]{3,0,2,1:T(1,128)S(1)} %get-tuple-element.225), channel_id=1, source_target_pairs={{1,0},{2,1},{3,2},{5,4},{6,5},{7,6},{9,8},{10,9},{11,10},{13,12},{... | collective-permute-start | bytes 728 | tf_op jit(solution)/shard_map/ppermute | solution.py:40
  447.0 11.3 %collective-permute-start.65 = (f32[1,10,6,1]{3,0,2,1:T(1,128)S(1)}, f32[1,10,6,1]{3,0,2,1:T(1,128)S(1)}, u32[]{:S(2)}, u32[]{:S(2)}) collective-permute-start(f32[1,10,6,1]{3,0,2,1:T(1,128)S(1)} %get-tuple-element.226), channel_id=1, source_target_pairs={{0,1},{1,2},{2,3},{4,5},{5,6},{6,7},{8,9},{9,10},{10,11},{12,13},{... | collective-permute-start | bytes 728 | tf_op jit(solution)/shard_map/ppermute | solution.py:38
  451.4 14.5 %collective-permute-start.142 = (f32[1,18,10,1]{3,0,2,1:T(1,128)S(1)}, f32[1,18,10,1]{3,0,2,1:T(1,128)S(1)}, u32[]{:S(2)}, u32[]{:S(2)}) collective-permute-start(f32[1,18,10,1]{3,0,2,1:T(1,128)S(1)} %get-tuple-element.151), channel_id=1, source_target_pairs={{1,0},{2,1},{3,2},{5,4},{6,5},{7,6},{9,8},{10,9},{11,10},{13,12},{... | collective-permute-start | bytes 2168 | tf_op jit(solution)/shard_map/ppermute | solution.py:40
  452.7 13.2 %collective-permute-start.143 = (f32[1,18,10,1]{3,0,2,1:T(1,128)S(1)}, f32[1,18,10,1]{3,0,2,1:T(1,128)S(1)}, u32[]{:S(2)}, u32[]{:S(2)}) collective-permute-start(f32[1,18,10,1]{3,0,2,1:T(1,128)S(1)} %get-tuple-element.152), channel_id=1, source_target_pairs={{0,1},{1,2},{2,3},{4,5},{5,6},{6,7},{8,9},{9,10},{10,11},{12,13},{... | collective-permute-start | bytes 2168 | tf_op jit(solution)/shard_map/ppermute | solution.py:38
  480.8 12.0 %collective-permute-start.72 = (f32[1,1,2,64]{3,1,2,0:T(1,128)S(1)}, f32[1,1,2,64]{3,1,2,0:T(1,128)S(1)}, u32[]{:S(2)}, u32[]{:S(2)}) collective-permute-start(f32[1,1,2,64]{3,1,2,0:T(1,128)S(1)} %get-tuple-element.338), channel_id=1, source_target_pairs={{8,0},{16,8},{24,16},{9,1},{17,9},{25,17},{10,2},{18,10},{26,18},{... | collective-permute-start | bytes 1544 | tf_op jit(solution)/shard_map/ppermute | solution.py:40
  482.1 10.7 %collective-permute-start.73 = (f32[1,1,2,64]{3,1,2,0:T(1,128)S(1)}, f32[1,1,2,64]{3,1,2,0:T(1,128)S(1)}, u32[]{:S(2)}, u32[]{:S(2)}) collective-permute-start(f32[1,1,2,64]{3,1,2,0:T(1,128)S(1)} %get-tuple-element.337), channel_id=1, source_target_pairs={{0,8},{8,16},{16,24},{1,9},{9,17},{17,25},{2,10},{10,18},{18,26},{... | collective-permute-start | bytes 1544 | tf_op jit(solution)/shard_map/ppermute | solution.py:38
  486.9 11.8 %collective-permute-start.144 = (f32[1,1,8,256]{3,2,1,0:T(8,128)S(1)}, f32[1,1,8,256]{3,2,1,0:T(8,128)S(1)}, u32[]{:S(2)}, u32[]{:S(2)}) collective-permute-start(f32[1,1,8,256]{3,2,1,0:T(8,128)S(1)} %get-tuple-element.206), channel_id=1, source_target_pairs={{8,0},{16,8},{24,16},{9,1},{17,9},{25,17},{10,2},{18,10},{26,18},{... | collective-permute-start | bytes 24584 | tf_op jit(solution)/shard_map/ppermute | solution.py:40
  488.2 10.5 %collective-permute-start.145 = (f32[1,1,8,256]{3,2,1,0:T(8,128)S(1)}, f32[1,1,8,256]{3,2,1,0:T(8,128)S(1)}, u32[]{:S(2)}, u32[]{:S(2)}) collective-permute-start(f32[1,1,8,256]{3,2,1,0:T(8,128)S(1)} %get-tuple-element.205), channel_id=1, source_target_pairs={{0,8},{8,16},{16,24},{1,9},{9,17},{17,25},{2,10},{10,18},{18,26},{... | collective-permute-start | bytes 24584 | tf_op jit(solution)/shard_map/ppermute | solution.py:38
  507.2 11.5 %collective-permute-start.78 = (f32[1,1,2,64]{3,1,2,0:T(1,128)S(1)}, f32[1,1,2,64]{3,1,2,0:T(1,128)S(1)}, u32[]{:S(2)}, u32[]{:S(2)}) collective-permute-start(f32[1,1,2,64]{3,1,2,0:T(1,128)S(1)} %get-tuple-element.336), channel_id=1, source_target_pairs={{8,0},{16,8},{24,16},{9,1},{17,9},{25,17},{10,2},{18,10},{26,18},{... | collective-permute-start | bytes 1544 | tf_op jit(solution)/shard_map/ppermute | solution.py:40
  508.5 10.3 %collective-permute-start.79 = (f32[1,1,2,64]{3,1,2,0:T(1,128)S(1)}, f32[1,1,2,64]{3,1,2,0:T(1,128)S(1)}, u32[]{:S(2)}, u32[]{:S(2)}) collective-permute-start(f32[1,1,2,64]{3,1,2,0:T(1,128)S(1)} %get-tuple-element.335), channel_id=1, source_target_pairs={{0,8},{8,16},{16,24},{1,9},{9,17},{17,25},{2,10},{10,18},{18,26},{... | collective-permute-start | bytes 1544 | tf_op jit(solution)/shard_map/ppermute | solution.py:38
  513.2 11.4 %collective-permute-start.147 = (f32[1,18,1,256]{3,2,1,0:T(1,128)S(1)}, f32[1,18,1,256]{3,2,1,0:T(1,128)S(1)}, u32[]{:S(2)}, u32[]{:S(2)}) collective-permute-start(f32[1,18,1,256]{3,2,1,0:T(1,128)S(1)} %get-tuple-element.174), channel_id=1, source_target_pairs={{0,4},{1,5},{2,6},{3,7},{8,12},{9,13},{10,14},{11,15},{16,20},{17,... | collective-permute-start | bytes 55304 | tf_op jit(solution)/shard_map/ppermute | solution.py:38
  533.4 12.2 %collective-permute-start.84 = (f32[1,1,4,128]{3,2,1,0:T(4,128)S(1)}, f32[1,1,4,128]{3,2,1,0:T(4,128)S(1)}, u32[]{:S(2)}, u32[]{:S(2)}) collective-permute-start(f32[1,1,4,128]{3,2,1,0:T(4,128)S(1)} %get-tuple-element.270), channel_id=1, source_target_pairs={{8,0},{16,8},{24,16},{9,1},{17,9},{25,17},{10,2},{18,10},{26,18},{... | collective-permute-start | bytes 6152 | tf_op jit(solution)/shard_map/ppermute | solution.py:40
  534.7 10.9 %collective-permute-start.85 = (f32[1,1,4,128]{3,2,1,0:T(4,128)S(1)}, f32[1,1,4,128]{3,2,1,0:T(4,128)S(1)}, u32[]{:S(2)}, u32[]{:S(2)}) collective-permute-start(f32[1,1,4,128]{3,2,1,0:T(4,128)S(1)} %get-tuple-element.269), channel_id=1, source_target_pairs={{0,8},{8,16},{16,24},{1,9},{9,17},{17,25},{2,10},{10,18},{18,26},{... | collective-permute-start | bytes 6152 | tf_op jit(solution)/shard_map/ppermute | solution.py:38
  539.5 11.9 %collective-permute-start.148 = (f32[1,18,10,1]{3,0,2,1:T(1,128)S(1)}, f32[1,18,10,1]{3,0,2,1:T(1,128)S(1)}, u32[]{:S(2)}, u32[]{:S(2)}) collective-permute-start(f32[1,18,10,1]{3,0,2,1:T(1,128)S(1)} %get-tuple-element.147), channel_id=1, source_target_pairs={{1,0},{2,1},{3,2},{5,4},{6,5},{7,6},{9,8},{10,9},{11,10},{13,12},{... | collective-permute-start | bytes 2168 | tf_op jit(solution)/shard_map/ppermute | solution.py:40
  540.8 10.7 %collective-permute-start.149 = (f32[1,18,10,1]{3,0,2,1:T(1,128)S(1)}, f32[1,18,10,1]{3,0,2,1:T(1,128)S(1)}, u32[]{:S(2)}, u32[]{:S(2)}) collective-permute-start(f32[1,18,10,1]{3,0,2,1:T(1,128)S(1)} %get-tuple-element.148), channel_id=1, source_target_pairs={{0,1},{1,2},{2,3},{4,5},{5,6},{6,7},{8,9},{9,10},{10,11},{12,13},{... | collective-permute-start | bytes 2168 | tf_op jit(solution)/shard_map/ppermute | solution.py:38
  553.0 18.3 %collective-permute-start.88 = (f32[1,10,6,1]{3,0,2,1:T(1,128)S(1)}, f32[1,10,6,1]{3,0,2,1:T(1,128)S(1)}, u32[]{:S(2)}, u32[]{:S(2)}) collective-permute-start(f32[1,10,6,1]{3,0,2,1:T(1,128)S(1)} %get-tuple-element.221), channel_id=1, source_target_pairs={{1,0},{2,1},{3,2},{5,4},{6,5},{7,6},{9,8},{10,9},{11,10},{13,12},{... | collective-permute-start | bytes 728 | tf_op jit(solution)/shard_map/ppermute | solution.py:40
  554.3 17.1 %collective-permute-start.89 = (f32[1,10,6,1]{3,0,2,1:T(1,128)S(1)}, f32[1,10,6,1]{3,0,2,1:T(1,128)S(1)}, u32[]{:S(2)}, u32[]{:S(2)}) collective-permute-start(f32[1,10,6,1]{3,0,2,1:T(1,128)S(1)} %get-tuple-element.222), channel_id=1, source_target_pairs={{0,1},{1,2},{2,3},{4,5},{5,6},{6,7},{8,9},{9,10},{10,11},{12,13},{... | collective-permute-start | bytes 728 | tf_op jit(solution)/shard_map/ppermute | solution.py:38
  644.8 12.0 %collective-permute-start.170 = (f32[1,6,1,64]{3,1,2,0:T(8,128)S(1)}, f32[1,6,1,64]{3,1,2,0:T(8,128)S(1)}, u32[]{:S(2)}, u32[]{:S(2)}) collective-permute-start(f32[1,6,1,64]{3,1,2,0:T(8,128)S(1)} %get-tuple-element.324), channel_id=1, source_target_pairs={{4,0},{5,1},{6,2},{7,3},{12,8},{13,9},{14,10},{15,11},{20,16},{21,... | collective-permute-start | bytes 4616 | tf_op jit(solution)/shard_map/ppermute | solution.py:40
  646.1 10.7 %collective-permute-start.171 = (f32[1,6,1,64]{3,1,2,0:T(8,128)S(1)}, f32[1,6,1,64]{3,1,2,0:T(8,128)S(1)}, u32[]{:S(2)}, u32[]{:S(2)}) collective-permute-start(f32[1,6,1,64]{3,1,2,0:T(8,128)S(1)} %get-tuple-element.323), channel_id=1, source_target_pairs={{0,4},{1,5},{2,6},{3,7},{8,12},{9,13},{10,14},{11,15},{16,20},{17,... | collective-permute-start | bytes 4616 | tf_op jit(solution)/shard_map/ppermute | solution.py:38
  650.7 19.5 %collective-permute-start.90 = (f32[1,1,8,256]{3,2,1,0:T(8,128)S(1)}, f32[1,1,8,256]{3,2,1,0:T(8,128)S(1)}, u32[]{:S(2)}, u32[]{:S(2)}) collective-permute-start(f32[1,1,8,256]{3,2,1,0:T(8,128)S(1)} %get-tuple-element.192), channel_id=1, source_target_pairs={{8,0},{16,8},{24,16},{9,1},{17,9},{25,17},{10,2},{18,10},{26,18},{... | collective-permute-start | bytes 24584 | tf_op jit(solution)/shard_map/ppermute | solution.py:40
  652.0 18.2 %collective-permute-start.91 = (f32[1,1,8,256]{3,2,1,0:T(8,128)S(1)}, f32[1,1,8,256]{3,2,1,0:T(8,128)S(1)}, u32[]{:S(2)}, u32[]{:S(2)}) collective-permute-start(f32[1,1,8,256]{3,2,1,0:T(8,128)S(1)} %get-tuple-element.191), channel_id=1, source_target_pairs={{0,8},{8,16},{16,24},{1,9},{9,17},{17,25},{2,10},{10,18},{18,26},{... | collective-permute-start | bytes 24584 | tf_op jit(solution)/shard_map/ppermute | solution.py:38
  678.8 10.2 %collective-permute-start.178 = (f32[1,10,6,1]{3,0,2,1:T(1,128)S(1)}, f32[1,10,6,1]{3,0,2,1:T(1,128)S(1)}, u32[]{:S(2)}, u32[]{:S(2)}) collective-permute-start(f32[1,10,6,1]{3,0,2,1:T(1,128)S(1)} %get-tuple-element.237), channel_id=1, source_target_pairs={{1,0},{2,1},{3,2},{5,4},{6,5},{7,6},{9,8},{10,9},{11,10},{13,12},{... | collective-permute-start | bytes 728 | tf_op jit(solution)/shard_map/ppermute | solution.py:40
  680.1 8.9 collective-permute-start.179
  683.2 13.1 %collective-permute-start.92 = (f32[1,18,1,256]{3,2,1,0:T(1,128)S(1)}, f32[1,18,1,256]{3,2,1,0:T(1,128)S(1)}, u32[]{:S(2)}, u32[]{:S(2)}) collective-permute-start(f32[1,18,1,256]{3,2,1,0:T(1,128)S(1)} %get-tuple-element.162), channel_id=1, source_target_pairs={{4,0},{5,1},{6,2},{7,3},{12,8},{13,9},{14,10},{15,11},{20,16},{21,... | collective-permute-start | bytes 55304 | tf_op jit(solution)/shard_map/ppermute | solution.py:40
  684.5 11.8 %collective-permute-start.93 = (f32[1,18,1,256]{3,2,1,0:T(1,128)S(1)}, f32[1,18,1,256]{3,2,1,0:T(1,128)S(1)}, u32[]{:S(2)}, u32[]{:S(2)}) collective-permute-start(f32[1,18,1,256]{3,2,1,0:T(1,128)S(1)} %get-tuple-element.161), channel_id=1, source_target_pairs={{0,4},{1,5},{2,6},{3,7},{8,12},{9,13},{10,14},{11,15},{16,20},{17,... | collective-permute-start | bytes 55304 | tf_op jit(solution)/shard_map/ppermute | solution.py:38
  697.7 10.6 %collective-permute-start.182 = (f32[1,18,1,256]{3,2,1,0:T(1,128)S(1)}, f32[1,18,1,256]{3,2,1,0:T(1,128)S(1)}, u32[]{:S(2)}, u32[]{:S(2)}) collective-permute-start(f32[1,18,1,256]{3,2,1,0:T(1,128)S(1)} %get-tuple-element.172), channel_id=1, source_target_pairs={{4,0},{5,1},{6,2},{7,3},{12,8},{13,9},{14,10},{15,11},{20,16},{21,... | collective-permute-start | bytes 55304 | tf_op jit(solution)/shard_map/ppermute | solution.py:40
  699.0 9.3 collective-permute-start.183
  703.8 11.0 %collective-permute-start.94 = (f32[1,18,10,1]{3,0,2,1:T(1,128)S(1)}, f32[1,18,10,1]{3,0,2,1:T(1,128)S(1)}, u32[]{:S(2)}, u32[]{:S(2)}) collective-permute-start(f32[1,18,10,1]{3,0,2,1:T(1,128)S(1)} %get-tuple-element.123), channel_id=1, source_target_pairs={{1,0},{2,1},{3,2},{5,4},{6,5},{7,6},{9,8},{10,9},{11,10},{13,12},{... | collective-permute-start | bytes 2168 | tf_op jit(solution)/shard_map/ppermute | solution.py:40
  705.1 9.7 collective-permute-start.95
  726.6 7.5 collective-permute-start.188
  (129 other events, 838.8 us)
